TPU v7x, 768 devices: a whole 4x8x12 slice. The times are simulated.
768 devices in a mesh: inner: 48 (over y, z_lo), outer: 16 (over x, z_hi, core).
Axes of the slice: x: 4, y: 8, z: 12 (z_hi: 2, z_lo: 6; z = z_hi * 6 + z_lo), core: 2. Of those that a mesh axis runs over, the one named last changes fastest.
Arguments:
- mentor_picture_vectors: bfloat16 [196608, 1152], P(('inner', 'outer')), may hold values from -1 to 1
- learner_picture_vectors: bfloat16 [196608, 768], P(('inner', 'outer')), may hold values from -1 to 1
- mentor_caption_vectors: bfloat16 [196608, 1152], P(('inner', 'outer')), may hold values from -1 to 1
- learner_caption_vectors: bfloat16 [196608, 768], P(('inner', 'outer')), may hold values from -1 to 1
- matching_round_lookup: int32 [196608], P(('inner', 'outer')), may hold values from 0 to 4
- sharpness_factor: float32 [], replicated, may hold values from 2 to 8
- learned_offset: float32 [], replicated, may hold values from -3 to -1
Outputs:
- image_grad: float32 [196608, 768], P(('inner', 'outer'))
- text_grad: float32 [196608, 768], P(('inner', 'outer'))
All inputs are finite; a program needn't handle non-finite values.
Results may differ from a plain program's by a relative error of at most 0.0018.
Values may be sent and summed in bfloat16 or wider, within the bound.
A program may use at most 32 MiB of HBM per device.

v0:
```python
import jax
import jax.numpy as jnp
from jax import lax
from jax.sharding import PartitionSpec as P

INNER_STEPS = 4
CAPTION_SLAB_NUM = 5


def shifted(block, axis, distance):
    devices = range(lax.axis_size(axis))
    route = [((i - distance) % len(devices), i) for i in devices]
    return lax.ppermute(block, axis, route)


def round_loss_pieces(
    mentor_picture_embedding,
    learner_picture_embedding,
    mentor_caption_embedding,
    learner_caption_embedding,
    desired_signs,
    round_tally,
    sharpness_factor,
    learned_offset,
):
    teacher = jnp.dot(
        mentor_picture_embedding, mentor_caption_embedding.T, preferred_element_type=jnp.float32
    )
    prob = jax.nn.sigmoid(4.0 * teacher - 2.0)
    learner_network = (
        sharpness_factor
        * jnp.dot(
            learner_picture_embedding,
            learner_caption_embedding.T,
            preferred_element_type=jnp.float32,
        )
        + learned_offset
    )
    rows = mentor_picture_embedding.shape[0]
    diag = jnp.eye(rows, dtype=jnp.float32)
    hits = (desired_signs == round_tally).astype(jnp.float32)
    target = 0.5 * (hits[:, None] * diag + prob)
    grad = (jax.nn.sigmoid(learner_network) - target).astype(jnp.bfloat16)
    picture_shard = jnp.dot(grad, learner_caption_embedding, preferred_element_type=jnp.float32)
    caption_shard = lax.dot_general(
        grad,
        learner_picture_embedding,
        (((0,), (0,)), ((), ())),
        preferred_element_type=jnp.float32,
    )
    return (picture_shard, caption_shard)


def shards(
    mentor_picture_vectors,
    learner_picture_vectors,
    mentor_caption_vectors,
    learner_caption_vectors,
    matching_round_lookup,
    sharpness_factor,
    learned_offset,
):
    img_grad = jnp.zeros(learner_picture_vectors.shape, jnp.float32)
    partials = []
    carried = None
    travelling_teacher = mentor_caption_vectors
    travelling_student = learner_caption_vectors
    for round_tally in range(INNER_STEPS):
        picture_shard, caption_shard = round_loss_pieces(
            mentor_picture_vectors,
            learner_picture_vectors,
            travelling_teacher,
            travelling_student,
            matching_round_lookup,
            round_tally,
            sharpness_factor,
            learned_offset,
        )
        img_grad = img_grad + picture_shard
        partials.append(caption_shard)
        carried = caption_shard if round_tally == 0 else carried + caption_shard
        if round_tally < INNER_STEPS - 1:
            carried = shifted(carried, "inner", 1)
        if round_tally < INNER_STEPS - 1:
            travelling_teacher, travelling_student = shifted(
                (travelling_teacher, travelling_student), "inner", 1
            )
    travelling_teacher, travelling_student = shifted(
        (travelling_teacher, travelling_student), "outer", 1
    )
    carried = shifted(carried, "outer", 1)
    picture_shard, caption_shard = round_loss_pieces(
        mentor_picture_vectors,
        learner_picture_vectors,
        travelling_teacher,
        travelling_student,
        matching_round_lookup,
        INNER_STEPS,
        sharpness_factor,
        learned_offset,
    )
    img_grad = img_grad + picture_shard
    carried = carried + caption_shard
    affinity_multiplier = sharpness_factor / CAPTION_SLAB_NUM
    return (affinity_multiplier * img_grad, affinity_multiplier * carried)


def solution(mesh):
    placed = (
        P(("inner", "outer"), None),
        P(("inner", "outer"), None),
        P(("inner", "outer"), None),
        P(("inner", "outer"), None),
        P(("inner", "outer")),
        P(),
        P(),
    )
    return jax.shard_map(
        shards,
        mesh=mesh,
        in_specs=placed,
        out_specs=(P(("inner", "outer"), None), P(("inner", "outer"), None)),
        check_vma=False,
    )
```

profile of v0, /device:TPU:216, one launch (start us, length us, event | category | flops | bytes accessed | tf_op | source)
XLA Modules:
  0.0 192.8 jit_solution(6920517805965096219)
XLA Ops:
  0.6 5.6 %collective-permute-start.1 = (bf16[256,1152]{1,0:T(8,128)(2,1)}, bf16[256,1152]{1,0:T(8,128)(2,1)}, u32[]{:S(2)}, u32[]{:S(2)}) collective-permute-start(bf16[256,1152]{1,0:T(8,128)(2,1)} %param.9), channel_id=1, source_target_pairs={{752,0},{0,16},{16,32},{32,48},{48,64},{64,80},{80,96},{96,112},{1... | collective-permute-start | bytes 1769480 | tf_op jit(solution)/shard_map/ppermute | solution.py:13
  6.3 4.3 %collective-permute-start = (bf16[256,768]{1,0:T(8,128)(2,1)}, bf16[256,768]{1,0:T(8,128)(2,1)S(1)}, u32[]{:S(2)}, u32[]{:S(2)}) collective-permute-start(bf16[256,768]{1,0:T(8,128)(2,1)} %param.10), channel_id=1, source_target_pairs={{752,0},{0,16},{16,32},{32,48},{48,64},{64,80},{80,96},{96,112},{1... | collective-permute-start | bytes 1179656 | tf_op jit(solution)/shard_map/ppermute | solution.py:13
  10.6 0.7 compare_convert_fusion
  12.6 1.5 fusion.65
  14.8 1.9 collective-permute-start.8
  17.0 11.7 %collective-permute-done = bf16[256,768]{1,0:T(8,128)(2,1)S(1)} collective-permute-done((bf16[256,768]{1,0:T(8,128)(2,1)}, bf16[256,768]{1,0:T(8,128)(2,1)S(1)}, u32[]{:S(2)}, u32[]{:S(2)}) %collective-permute-start) | collective-permute-done | bytes 393248 | tf_op jit(solution)/shard_map/ppermute | solution.py:13
  28.7 5.5 %collective-permute-start.2 = (bf16[256,768]{1,0:T(8,128)(2,1)S(1)}, bf16[256,768]{1,0:T(8,128)(2,1)S(1)}, u32[]{:S(2)}, u32[]{:S(2)}) collective-permute-start(bf16[256,768]{1,0:T(8,128)(2,1)S(1)} %collective-permute-done), channel_id=1, source_target_pairs={{752,0},{0,16},{16,32},{32,48},{48,64},{64,80},{80,96},{96,112},{1... | collective-permute-start | bytes 1179656 | tf_op jit(solution)/shard_map/ppermute | solution.py:13
  34.2 3.1 %collective-permute-start.3 = (bf16[256,1152]{1,0:T(8,128)(2,1)}, bf16[256,1152]{1,0:T(8,128)(2,1)S(1)}, u32[]{:S(2)}, u32[]{:S(2)}) collective-permute-start(bf16[256,1152]{1,0:T(8,128)(2,1)} %collective-permute-done.1), channel_id=1, source_target_pairs={{752,0},{0,16},{16,32},{32,48},{48,64},{64,80},{80,96},{96,112},{1... | collective-permute-start | bytes 1769480 | tf_op jit(solution)/shard_map/ppermute | solution.py:13
  37.3 1.5 fusion.58
  38.8 0.4 fusion.67
  39.4 6.0 %collective-permute-done.8 = f32[256,768]{1,0:T(8,128)S(1)} collective-permute-done((f32[256,768]{1,0:T(8,128)S(1)}, f32[256,768]{1,0:T(8,128)S(1)}, u32[]{:S(2)}, u32[]{:S(2)}) %collective-permute-start.8) | collective-permute-done | bytes 786464 | tf_op jit(solution)/shard_map/ppermute | solution.py:13
  45.8 5.6 %collective-permute-start.9 = (f32[256,768]{1,0:T(8,128)S(1)}, f32[256,768]{1,0:T(8,128)S(1)}, u32[]{:S(2)}, u32[]{:S(2)}) collective-permute-start(f32[256,768]{1,0:T(8,128)S(1)} %convolution_add_fusion), channel_id=1, source_target_pairs={{752,0},{0,16},{16,32},{32,48},{48,64},{64,80},{80,96},{96,112},{1... | collective-permute-start | bytes 2359304 | tf_op jit(solution)/shard_map/ppermute | solution.py:13
  51.4 2.5 %collective-permute-done.2 = bf16[256,768]{1,0:T(8,128)(2,1)S(1)} collective-permute-done((bf16[256,768]{1,0:T(8,128)(2,1)S(1)}, bf16[256,768]{1,0:T(8,128)(2,1)S(1)}, u32[]{:S(2)}, u32[]{:S(2)}) %collective-permute-start.2) | collective-permute-done | bytes 393248 | tf_op jit(solution)/shard_map/ppermute | solution.py:13
  53.9 5.6 %collective-permute-start.4 = (bf16[256,768]{1,0:T(8,128)(2,1)S(1)}, bf16[256,768]{1,0:T(8,128)(2,1)S(1)}, u32[]{:S(2)}, u32[]{:S(2)}) collective-permute-start(bf16[256,768]{1,0:T(8,128)(2,1)S(1)} %collective-permute-done.2), channel_id=1, source_target_pairs={{752,0},{0,16},{16,32},{32,48},{48,64},{64,80},{80,96},{96,112},{1... | collective-permute-start | bytes 1179656 | tf_op jit(solution)/shard_map/ppermute | solution.py:13
  59.5 7.1 %collective-permute-done.3 = bf16[256,1152]{1,0:T(8,128)(2,1)S(1)} collective-permute-done((bf16[256,1152]{1,0:T(8,128)(2,1)}, bf16[256,1152]{1,0:T(8,128)(2,1)S(1)}, u32[]{:S(2)}, u32[]{:S(2)}) %collective-permute-start.3) | collective-permute-done | bytes 589856 | tf_op jit(solution)/shard_map/ppermute | solution.py:13
  66.7 5.5 %collective-permute-start.5 = (bf16[256,1152]{1,0:T(8,128)(2,1)S(1)}, bf16[256,1152]{1,0:T(8,128)(2,1)S(1)}, u32[]{:S(2)}, u32[]{:S(2)}) collective-permute-start(bf16[256,1152]{1,0:T(8,128)(2,1)S(1)} %collective-permute-done.3), channel_id=1, source_target_pairs={{752,0},{0,16},{16,32},{32,48},{48,64},{64,80},{80,96},{96,112},{1... | collective-permute-start | bytes 1769480 | tf_op jit(solution)/shard_map/ppermute | solution.py:13
  72.1 0.4 fusion.51
  72.6 0.4 fusion.68
  72.9 18.9 %collective-permute-done.4 = bf16[256,768]{1,0:T(8,128)(2,1)S(1)} collective-permute-done((bf16[256,768]{1,0:T(8,128)(2,1)S(1)}, bf16[256,768]{1,0:T(8,128)(2,1)S(1)}, u32[]{:S(2)}, u32[]{:S(2)}) %collective-permute-start.4) | collective-permute-done | bytes 393248 | tf_op jit(solution)/shard_map/ppermute | solution.py:13
  91.8 1.9 collective-permute-start.6
  94.4 5.6 %collective-permute-start.10 = (f32[256,768]{1,0:T(8,128)S(1)}, f32[256,768]{1,0:T(8,128)S(1)}, u32[]{:S(2)}, u32[]{:S(2)}) collective-permute-start(f32[256,768]{1,0:T(8,128)S(1)} %add.122), channel_id=1, source_target_pairs={{752,0},{0,16},{16,32},{32,48},{48,64},{64,80},{80,96},{96,112},{1... | collective-permute-start | bytes 2359304 | tf_op jit(solution)/shard_map/ppermute | solution.py:13
  100.0 3.3 %collective-permute-done.5 = bf16[256,1152]{1,0:T(8,128)(2,1)S(1)} collective-permute-done((bf16[256,1152]{1,0:T(8,128)(2,1)S(1)}, bf16[256,1152]{1,0:T(8,128)(2,1)S(1)}, u32[]{:S(2)}, u32[]{:S(2)}) %collective-permute-start.5) | collective-permute-done | bytes 589856 | tf_op jit(solution)/shard_map/ppermute | solution.py:13
  103.3 6.3 %collective-permute-start.7 = (bf16[256,1152]{1,0:T(8,128)(2,1)S(1)}, bf16[256,1152]{1,0:T(8,128)(2,1)S(1)}, u32[]{:S(2)}, u32[]{:S(2)}) collective-permute-start(bf16[256,1152]{1,0:T(8,128)(2,1)S(1)} %collective-permute-done.5), channel_id=1, source_target_pairs={{15,0},{0,1},{1,2},{2,3},{3,4},{4,5},{5,6},{6,7},{7,8},{8,9},{9,10... | collective-permute-start | bytes 1769480 | tf_op jit(solution)/shard_map/ppermute | solution.py:13
  109.6 0.4 fusion.44
  110.0 0.4 fusion.69
  111.0 18.9 %collective-permute-done.10 = f32[256,768]{1,0:T(8,128)S(1)} collective-permute-done((f32[256,768]{1,0:T(8,128)S(1)}, f32[256,768]{1,0:T(8,128)S(1)}, u32[]{:S(2)}, u32[]{:S(2)}) %collective-permute-start.10) | collective-permute-done | bytes 786464 | tf_op jit(solution)/shard_map/ppermute | solution.py:13
  130.0 34.5 %collective-permute-start.11 = (f32[256,768]{1,0:T(8,128)S(1)}, f32[256,768]{1,0:T(8,128)S(1)}, u32[]{:S(2)}, u32[]{:S(2)}) collective-permute-start(f32[256,768]{1,0:T(8,128)S(1)} %add.123), channel_id=1, source_target_pairs={{15,0},{0,1},{1,2},{2,3},{3,4},{4,5},{5,6},{6,7},{7,8},{8,9},{9,10... | collective-permute-start | bytes 2359304 | tf_op jit(solution)/shard_map/ppermute | solution.py:13
  164.5 0.4 fusion.37
  164.9 0.4 fusion.70
  165.6 1.2 fusion
  166.8 25.1 %collective-permute-done.11 = f32[256,768]{1,0:T(8,128)S(1)} collective-permute-done((f32[256,768]{1,0:T(8,128)S(1)}, f32[256,768]{1,0:T(8,128)S(1)}, u32[]{:S(2)}, u32[]{:S(2)}) %collective-permute-start.11) | collective-permute-done | bytes 786464 | tf_op jit(solution)/shard_map/ppermute | solution.py:13
  191.9 1.0 add_multiply_fusion
  (22 shorter events, 3.1 us)
Async XLA Ops:
  0.6 11.9 %copy-start = (bf16[256,1152]{1,0:T(8,128)(2,1)S(1)}, bf16[256,1152]{1,0:T(8,128)(2,1)}, u32[]{:S(2)}) copy-start(bf16[256,1152]{1,0:T(8,128)(2,1)} %param.7) | copy-start | bytes 1769476
  0.6 33.6 %collective-permute-start.1 = (bf16[256,1152]{1,0:T(8,128)(2,1)}, bf16[256,1152]{1,0:T(8,128)(2,1)}, u32[]{:S(2)}, u32[]{:S(2)}) collective-permute-start(bf16[256,1152]{1,0:T(8,128)(2,1)} %param.9), channel_id=1, source_target_pairs={{752,0},{0,16},{16,32},{32,48},{48,64},{64,80},{80,96},{96,112},{1... | collective-permute-start | bytes 1769480 | tf_op jit(solution)/shard_map/ppermute | solution.py:13
  6.3 22.5 %collective-permute-start = (bf16[256,768]{1,0:T(8,128)(2,1)}, bf16[256,768]{1,0:T(8,128)(2,1)S(1)}, u32[]{:S(2)}, u32[]{:S(2)}) collective-permute-start(bf16[256,768]{1,0:T(8,128)(2,1)} %param.10), channel_id=1, source_target_pairs={{752,0},{0,16},{16,32},{32,48},{48,64},{64,80},{80,96},{96,112},{1... | collective-permute-start | bytes 1179656 | tf_op jit(solution)/shard_map/ppermute | solution.py:13
  12.6 1.6 copy-start.1
  12.6 1.6 copy-start.2
  14.8 30.7 %collective-permute-start.8 = (f32[256,768]{1,0:T(8,128)S(1)}, f32[256,768]{1,0:T(8,128)S(1)}, u32[]{:S(2)}, u32[]{:S(2)}) collective-permute-start(f32[256,768]{1,0:T(8,128)S(1)} %fusion.72), channel_id=1, source_target_pairs={{752,0},{0,16},{16,32},{32,48},{48,64},{64,80},{80,96},{96,112},{1... | collective-permute-start | bytes 2359304 | tf_op jit(solution)/shard_map/ppermute | solution.py:13
  28.7 25.2 %collective-permute-start.2 = (bf16[256,768]{1,0:T(8,128)(2,1)S(1)}, bf16[256,768]{1,0:T(8,128)(2,1)S(1)}, u32[]{:S(2)}, u32[]{:S(2)}) collective-permute-start(bf16[256,768]{1,0:T(8,128)(2,1)S(1)} %collective-permute-done), channel_id=1, source_target_pairs={{752,0},{0,16},{16,32},{32,48},{48,64},{64,80},{80,96},{96,112},{1... | collective-permute-start | bytes 1179656 | tf_op jit(solution)/shard_map/ppermute | solution.py:13
  34.2 32.4 %collective-permute-start.3 = (bf16[256,1152]{1,0:T(8,128)(2,1)}, bf16[256,1152]{1,0:T(8,128)(2,1)S(1)}, u32[]{:S(2)}, u32[]{:S(2)}) collective-permute-start(bf16[256,1152]{1,0:T(8,128)(2,1)} %collective-permute-done.1), channel_id=1, source_target_pairs={{752,0},{0,16},{16,32},{32,48},{48,64},{64,80},{80,96},{96,112},{1... | collective-permute-start | bytes 1769480 | tf_op jit(solution)/shard_map/ppermute | solution.py:13
  45.8 48.5 %collective-permute-start.9 = (f32[256,768]{1,0:T(8,128)S(1)}, f32[256,768]{1,0:T(8,128)S(1)}, u32[]{:S(2)}, u32[]{:S(2)}) collective-permute-start(f32[256,768]{1,0:T(8,128)S(1)} %convolution_add_fusion), channel_id=1, source_target_pairs={{752,0},{0,16},{16,32},{32,48},{48,64},{64,80},{80,96},{96,112},{1... | collective-permute-start | bytes 2359304 | tf_op jit(solution)/shard_map/ppermute | solution.py:13
  53.9 37.9 %collective-permute-start.4 = (bf16[256,768]{1,0:T(8,128)(2,1)S(1)}, bf16[256,768]{1,0:T(8,128)(2,1)S(1)}, u32[]{:S(2)}, u32[]{:S(2)}) collective-permute-start(bf16[256,768]{1,0:T(8,128)(2,1)S(1)} %collective-permute-done.2), channel_id=1, source_target_pairs={{752,0},{0,16},{16,32},{32,48},{48,64},{64,80},{80,96},{96,112},{1... | collective-permute-start | bytes 1179656 | tf_op jit(solution)/shard_map/ppermute | solution.py:13
  66.7 36.7 %collective-permute-start.5 = (bf16[256,1152]{1,0:T(8,128)(2,1)S(1)}, bf16[256,1152]{1,0:T(8,128)(2,1)S(1)}, u32[]{:S(2)}, u32[]{:S(2)}) collective-permute-start(bf16[256,1152]{1,0:T(8,128)(2,1)S(1)} %collective-permute-done.3), channel_id=1, source_target_pairs={{752,0},{0,16},{16,32},{32,48},{48,64},{64,80},{80,96},{96,112},{1... | collective-permute-start | bytes 1769480 | tf_op jit(solution)/shard_map/ppermute | solution.py:13
  91.8 73.1 %collective-permute-start.6 = (bf16[256,768]{1,0:T(8,128)(2,1)S(1)}, bf16[256,768]{1,0:T(8,128)(2,1)S(1)}, u32[]{:S(2)}, u32[]{:S(2)}) collective-permute-start(bf16[256,768]{1,0:T(8,128)(2,1)S(1)} %collective-permute-done.4), channel_id=1, source_target_pairs={{15,0},{0,1},{1,2},{2,3},{3,4},{4,5},{5,6},{6,7},{7,8},{8,9},{9,10... | collective-permute-start | bytes 1179656 | tf_op jit(solution)/shard_map/ppermute | solution.py:13
  94.4 35.5 %collective-permute-start.10 = (f32[256,768]{1,0:T(8,128)S(1)}, f32[256,768]{1,0:T(8,128)S(1)}, u32[]{:S(2)}, u32[]{:S(2)}) collective-permute-start(f32[256,768]{1,0:T(8,128)S(1)} %add.122), channel_id=1, source_target_pairs={{752,0},{0,16},{16,32},{32,48},{48,64},{64,80},{80,96},{96,112},{1... | collective-permute-start | bytes 2359304 | tf_op jit(solution)/shard_map/ppermute | solution.py:13
  103.3 61.2 %collective-permute-start.7 = (bf16[256,1152]{1,0:T(8,128)(2,1)S(1)}, bf16[256,1152]{1,0:T(8,128)(2,1)S(1)}, u32[]{:S(2)}, u32[]{:S(2)}) collective-permute-start(bf16[256,1152]{1,0:T(8,128)(2,1)S(1)} %collective-permute-done.5), channel_id=1, source_target_pairs={{15,0},{0,1},{1,2},{2,3},{3,4},{4,5},{5,6},{6,7},{7,8},{8,9},{9,10... | collective-permute-start | bytes 1769480 | tf_op jit(solution)/shard_map/ppermute | solution.py:13
  130.0 61.9 %collective-permute-start.11 = (f32[256,768]{1,0:T(8,128)S(1)}, f32[256,768]{1,0:T(8,128)S(1)}, u32[]{:S(2)}, u32[]{:S(2)}) collective-permute-start(f32[256,768]{1,0:T(8,128)S(1)} %add.123), channel_id=1, source_target_pairs={{15,0},{0,1},{1,2},{2,3},{3,4},{4,5},{5,6},{6,7},{7,8},{8,9},{9,10... | collective-permute-start | bytes 2359304 | tf_op jit(solution)/shard_map/ppermute | solution.py:13
where the time goes:
time: 193 us
  waiting for transfers between devices  93.6 us (48%)
  starting transfers between devices  85.4 us (44%)
  matrix products  9.74 us (5%)
  between operations  2.25 us (1%)
    ppermute x12, waiting for transfers between devices, shifted(): return lax.ppermute(block, axis, route)  93.6 us
    ppermute x12, starting transfers between devices, shifted(): return lax.ppermute(block, axis, route)  85.4 us
    dot_general x5, matrix products, round_loss_pieces(): jnp.dot(mentor_picture_embedding, mentor_caption_embedding.T, preferred_e...  4.24 us
  transfers between devices with their start and end apart: 12, of which 8 were waited for; matrix products, arithmetic and copies ran while one was open for 5% of the time, Pallas kernels for 0%

commit v1 on v0

v1 whole, which is shorter than its diff:
```python
import jax
import jax.numpy as jnp
from jax import lax
from jax.experimental import pallas as pl
from jax.experimental.pallas import tpu as pltpu
from jax.sharding import PartitionSpec as P

STEPS = 5
WIRE = jnp.int16
TOP = 32000.0
MESH = pl.DeviceIdType.MESH


def kernel(n_inner, n_outer, scalars, mi, li, mt, lt, look, img_out, txt_out,
           tm, tl, im, il, lk, acc_img, acc_txt, gsend, grecv, msend, mrecv,
           lsem, tm_s, tl_s, tm_r, tl_r, i_s, i_r, g_s, g_r, m_s, m_r):
    i, o = lax.axis_index("inner"), lax.axis_index("outer")
    c = lax.rem(o, 2)
    at = lambda d: lax.rem(i + d + n_inner, n_inner)
    up, down = lax.rem(o + 1, n_outer), lax.rem(o + n_outer - 1, n_outer)
    rows = tm.shape[1]

    def copy(src, dst, ss, rs, dev):
        return pltpu.make_async_remote_copy(
            src_ref=src, dst_ref=dst, send_sem=ss, recv_sem=rs, device_id=dev, device_id_type=MESH)

    def signal(dev):
        pl.semaphore_signal(barrier, inc=1, device_id=dev, device_id_type=MESH)

    local = [
        pltpu.make_async_copy(mi, im.at[0], lsem.at[0]),
        pltpu.make_async_copy(li, il.at[0], lsem.at[1]),
        pltpu.make_async_copy(mt, tm.at[0], lsem.at[2]),
        pltpu.make_async_copy(lt, tl.at[0], lsem.at[3]),
        pltpu.make_async_copy(look, lk.at[0], lsem.at[4]),
    ]
    def text_next(k, dev):
        return (copy(tm.at[k], tm.at[k + 1], tm_s.at[k], tm_r.at[k + 1], dev),
                copy(tl.at[k], tl.at[k + 1], tl_s.at[k], tl_r.at[k + 1], dev))

    def text_last(k, dev):
        return (copy(tm.at[k], tm.at[4], tm_s.at[3], tm_r.at[4], dev),
                copy(tl.at[k], tl.at[4], tl_s.at[3], tl_r.at[4], dev))

    def image_back():
        dev = (at(-2), o)
        return (copy(im.at[0], im.at[1], i_s.at[0], i_r.at[0], dev),
                copy(il.at[0], il.at[1], i_s.at[1], i_r.at[1], dev),
                copy(lk.at[0], lk.at[1], i_s.at[2], i_r.at[2], dev))

    def grad(k, slot, dev):
        return (copy(msend.at[k], mrecv.at[slot], m_s.at[k], m_r.at[slot], dev),
                copy(gsend.at[k], grecv.at[slot], g_s.at[k], g_r.at[slot], dev))

    def send_grad(k, slot, dev, x):
        top = jnp.maximum(jnp.max(jnp.abs(x)), 1e-30)
        msend[k] = jnp.full(msend.shape[1:], top, jnp.float32)
        gsend[k] = jnp.round(x * (TOP / top)).astype(jnp.int32).astype(WIRE)
        for cp in grad(k, slot, dev):
            cp.start()

    def received(slot):
        for cp in grad(0, slot, (i, o)):
            cp.wait_recv()
        return grecv[slot].astype(jnp.int32).astype(jnp.float32) * (mrecv[slot, 0:1, 0:1] * (1.0 / TOP))

    for cp in local:
        cp.start()
    barrier = pltpu.get_barrier_semaphore()
    signal((at(-1), o))

    @pl.when(c == 0)
    def _():
        signal((at(-3), down))
        pl.semaphore_wait(barrier, 2)

    @pl.when(c == 1)
    def _():
        signal((at(2), o))
        signal((at(1), o))
        signal((at(-2), o))
        signal((i, down))
        pl.semaphore_wait(barrier, 5)

    for cp in local:
        cp.wait()
    for cp in text_next(0, (at(1), o)):
        cp.start()

    @pl.when(c == 1)
    def _():
        for cp in image_back():
            cp.start()
        for cp in text_last(0, (at(3), up)):
            cp.start()

    acc_img[...] = jnp.zeros_like(acc_img)
    acc_txt[...] = jnp.zeros_like(acc_txt)
    sharp, offset = scalars[0], scalars[1]

    def step(s, carry):
        u = lax.rem(s // 2, 2)
        a, b = c * u, s - 2 * c * u

        @pl.when((c == 0) & (s > 0) & (s < 3))
        def _():
            for w, cp in zip(text_next(s - 1, (i, o)), text_next(s, (at(1), o))):
                w.wait_recv()
                cp.start()

        @pl.when((c == 0) & (s == 3))
        def _():
            for w, cp in zip(text_next(2, (i, o)), text_last(3, (i, up))):
                w.wait_recv()
                cp.start()

        @pl.when((c == 1) & (s == 1))
        def _():
            for w in text_next(0, (i, o)):
                w.wait_recv()

        @pl.when((c == 1) & (s == 2))
        def _():
            for w in image_back():
                w.wait_recv()

        @pl.when(s == 4)
        def _():
            for w in text_last(0, (i, o)):
                w.wait_recv()

        dims = (((1,), (1,)), ((), ()))
        teacher = lax.dot_general(im[a], tm[b], dims, preferred_element_type=jnp.float32)
        prob = jax.nn.sigmoid(4.0 * teacher - 2.0)
        student = sharp * lax.dot_general(
            il[a], tl[b], dims, preferred_element_type=jnp.float32) + offset
        r = lax.broadcasted_iota(jnp.int32, (rows, rows), 0)
        q = lax.broadcasted_iota(jnp.int32, (rows, rows), 1)
        hit = (r == q) & (lk[a, 0:1, :] == s)
        target = 0.5 * (jnp.where(hit, 1.0, 0.0) + prob)
        g = (jax.nn.sigmoid(student) - target).astype(jnp.bfloat16)
        acc_img[a] += jnp.dot(g, tl[b], preferred_element_type=jnp.float32)
        acc_txt[b] += lax.dot_general(
            g, il[a], (((0,), (0,)), ((), ())), preferred_element_type=jnp.float32)

        @pl.when((c == 0) & (s == 0))
        def _():
            send_grad(0, 1, (at(1), o), acc_txt[0])

        @pl.when((c == 0) & (s > 0) & (s < 3))
        def _():
            send_grad(s, s + 1, (at(1), o), acc_txt[s] + received(s))

        @pl.when((c == 0) & (s == 3))
        def _():
            send_grad(3, 4, (i, up), acc_txt[3] + received(3))

        @pl.when((c == 1) & (s == 3))
        def _():
            send_grad(1, 1, (at(-1), o), acc_txt[1])
            send_grad(4, 0, (at(2), o), acc_img[1])
            send_grad(0, 4, (at(3), up), acc_txt[0] + received(1))

        return carry

    lax.fori_loop(0, STEPS, step, 0)
    scale = sharp / STEPS

    @pl.when(c == 0)
    def _():
        img_out[...] = scale * acc_img[0]

    @pl.when(c == 1)
    def _():
        img_out[...] = scale * (acc_img[0] + received(0))

    txt_out[...] = scale * (acc_txt[4] + received(4))

    def sent(copies):
        for cp in copies:
            cp.wait_send()

    sent(text_next(0, (i, o)) + text_last(0, (i, o)))
    sent(grad(0, 4, (i, o)) + grad(1, 4, (i, o)))

    @pl.when(c == 0)
    def _():
        sent(text_next(1, (i, o)) + text_next(2, (i, o)))
        sent(grad(2, 4, (i, o)) + grad(3, 4, (i, o)))

    @pl.when(c == 1)
    def _():
        sent(image_back() + grad(4, 0, (i, o)))


def solution(mesh):
    n_inner, n_outer = mesh.shape["inner"], mesh.shape["outer"]

    def shards(mi, li, mt, lt, lookup, sharpness, offset):
        rows, dt = mi.shape
        ds = li.shape[1]
        scalars = jnp.stack([sharpness, offset])
        look = jnp.broadcast_to(lookup[None, :], (8, rows))
        hbm = pl.BlockSpec(memory_space=pl.ANY)
        vmem = pl.BlockSpec(memory_space=pltpu.VMEM)
        bf, f32, dma = jnp.bfloat16, jnp.float32, pltpu.SemaphoreType.DMA
        return pl.pallas_call(
            lambda *refs: kernel(n_inner, n_outer, *refs),
            out_shape=(jax.ShapeDtypeStruct((rows, ds), f32), jax.ShapeDtypeStruct((rows, ds), f32)),
            in_specs=[pl.BlockSpec(memory_space=pltpu.SMEM)] + [hbm] * 5,
            out_specs=(vmem, vmem),
            scratch_shapes=[
                pltpu.VMEM((5, rows, dt), bf), pltpu.VMEM((5, rows, ds), bf),
                pltpu.VMEM((2, rows, dt), bf), pltpu.VMEM((2, rows, ds), bf),
                pltpu.VMEM((2, 8, rows), jnp.int32),
                pltpu.VMEM((2, rows, ds), f32), pltpu.VMEM((5, rows, ds), f32),
                pltpu.VMEM((5, rows, ds), WIRE), pltpu.VMEM((5, rows, ds), WIRE),
                pltpu.VMEM((5, 8, 128), f32), pltpu.VMEM((5, 8, 128), f32),
                dma((5,)), dma((4,)), dma((4,)), dma((5,)), dma((5,)),
                dma((3,)), dma((3,)), dma((5,)), dma((5,)), dma((5,)), dma((5,)),
            ],
            compiler_params=pltpu.CompilerParams(
                collective_id=0, has_side_effects=True, vmem_limit_bytes=48 * 2**20),
            cost_estimate=pl.CostEstimate(
                flops=STEPS * 4 * rows * rows * (dt + 3 * ds) // 2, bytes_accessed=8 * rows * (dt + 3 * ds),
                transcendentals=2 * STEPS * rows * rows),
        )(scalars, mi, li, mt, lt, look)

    row = P(("inner", "outer"), None)
    return jax.shard_map(
        shards, mesh=mesh,
        in_specs=(row, row, row, row, P(("inner", "outer")), P(), P()),
        out_specs=(row, row), check_vma=False)
```

time: 193 us -> 143 us (0.74)
  the two profiles are of different devices: /device:TPU:216 before, /device:TPU:1 now
where the time goes in v1:
time: 143 us; the launch traced here: 142 us
  Pallas kernels  134 us (94%)
  local copies, waits for them, and re-layouts  6.48 us (5%)
  between operations  1.94 us (1%)
    pallas_call x1, Pallas kernels, shards(): pl.pallas_call(lambda *refs: kernel(n_inner, n_outer, *refs), out_shape=(...  134 us
    unnamed x12, local copies, waits for them, and re-layouts  6.48 us

profile of v1, /device:TPU:1, one launch (start us, length us, event | category | flops | bytes accessed | tf_op | source)
XLA Modules:
  0.0 142.4 jit_solution(13631901303396759649)
XLA Ops:
  1.9 0.0 copy-start.4
  1.9 0.1 pad_maximum_fusion.refs_0_
  2.0 0.6 copy-done.4
  2.6 0.0 copy-start
  2.6 1.1 copy-done
  3.7 0.0 copy-start.1
  3.7 1.1 copy-done.1
  4.7 0.0 copy-start.2
  4.7 1.0 copy-done.2
  5.7 0.0 copy-start.3
  5.7 1.0 copy-done.3
  6.7 133.9 %shard_map.86 = (f32[256,768]{1,0:T(8,128)S(1)}, f32[256,768]{1,0:T(8,128)S(1)}) custom-call(f32[2]{0:T(128)S(1)} %pad_maximum_fusion.refs_0_, bf16[256,1152]{1,0:T(8,128)(2,1)S(1)} %copy-done, bf16[256,768]{1,0:T(8,128)(2,1)S(1)} %copy-done.2, bf16[256,1152]{1,0:T(8,128)(2,1)S(1)} %copy-done.1, bf16[256,768]{1,0:T(8,128)(2,1)S(1)} %copy-done.3, ...), custom_call_target="tpu_custom_call" | custom-call | flops 2264924160 | bytes 7077888 | tf_op jit(solution)/shard_map/pallas_call | solution.py:207
  140.6 0.9 copy.13
  141.5 0.9 copy.14
  (1 shorter events, 0.0 us)
Async XLA Ops:
  1.9 0.7 copy-start.4
  2.6 1.1 copy-start
  3.7 1.1 copy-start.1
  4.7 1.0 copy-start.2
  5.7 1.0 copy-start.3

commit v2 on v1

--- a/solution.py
+++ b/solution.py
@@ -8,6 +8,8 @@
 STEPS = 5
 WIRE = jnp.int16
 TOP = 32000.0
+PIECES = 2
+LATE = 1
 MESH = pl.DeviceIdType.MESH
 
 
@@ -34,13 +36,16 @@
         pltpu.make_async_copy(lt, tl.at[0], lsem.at[3]),
         pltpu.make_async_copy(look, lk.at[0], lsem.at[4]),
     ]
+    def text(k, to, sem, dev):
+        n = rows // PIECES
+        return [copy(buf.at[k, pl.ds(q * n, n)], buf.at[to, pl.ds(q * n, n)], ss.at[sem, q], rs.at[to, q], dev)
+                for buf, ss, rs in ((tm, tm_s, tm_r), (tl, tl_s, tl_r)) for q in range(PIECES)]
+
     def text_next(k, dev):
-        return (copy(tm.at[k], tm.at[k + 1], tm_s.at[k], tm_r.at[k + 1], dev),
-                copy(tl.at[k], tl.at[k + 1], tl_s.at[k], tl_r.at[k + 1], dev))
+        return text(k, k + 1, k, dev)
 
     def text_last(k, dev):
-        return (copy(tm.at[k], tm.at[4], tm_s.at[3], tm_r.at[4], dev),
-                copy(tl.at[k], tl.at[4], tl_s.at[3], tl_r.at[4], dev))
+        return text(k, 4, 3, dev)
 
     def image_back():
         dev = (at(-2), o)
@@ -91,8 +96,9 @@
     def _():
         for cp in image_back():
             cp.start()
-        for cp in text_last(0, (at(3), up)):
-            cp.start()
+        if LATE == 0:
+            for cp in text_last(0, (at(3), up)):
+                cp.start()
 
     acc_img[...] = jnp.zeros_like(acc_img)
     acc_txt[...] = jnp.zeros_like(acc_txt)
@@ -119,10 +125,19 @@
             for w in text_next(0, (i, o)):
                 w.wait_recv()
 
+        if LATE == 1:
+            @pl.when((c == 1) & (s == 1))
+            def _():
+                for cp in text_last(0, (at(3), up)):
+                    cp.start()
+
         @pl.when((c == 1) & (s == 2))
         def _():
             for w in image_back():
                 w.wait_recv()
+            if LATE == 2:
+                for cp in text_last(0, (at(3), up)):
+                    cp.start()
 
         @pl.when(s == 4)
         def _():
@@ -216,11 +231,11 @@
                 pltpu.VMEM((2, rows, ds), f32), pltpu.VMEM((5, rows, ds), f32),
                 pltpu.VMEM((5, rows, ds), WIRE), pltpu.VMEM((5, rows, ds), WIRE),
                 pltpu.VMEM((5, 8, 128), f32), pltpu.VMEM((5, 8, 128), f32),
-                dma((5,)), dma((4,)), dma((4,)), dma((5,)), dma((5,)),
+                dma((5,)), dma((4, PIECES)), dma((4, PIECES)), dma((5, PIECES)), dma((5, PIECES)),
                 dma((3,)), dma((3,)), dma((5,)), dma((5,)), dma((5,)), dma((5,)),
             ],
             compiler_params=pltpu.CompilerParams(
-                collective_id=0, has_side_effects=True, vmem_limit_bytes=48 * 2**20),
+                collective_id=0, has_side_effects=True, vmem_limit_bytes=60 * 2**20),
             cost_estimate=pl.CostEstimate(
                 flops=STEPS * 4 * rows * rows * (dt + 3 * ds) // 2, bytes_accessed=8 * rows * (dt + 3 * ds),
                 transcendentals=2 * STEPS * rows * rows),

time: 143 us -> 135 us (0.944); the launches traced: 142 us -> 133 us
  Pallas kernels: 134 us -> 126 us
  local copies, waits for them, and re-layouts: 6.48 us -> 3.64 us
    pallas_call x1, Pallas kernels: 134 us -> 126 us  [shards(): pl.pallas_call(lambda *refs: kernel(n_inner, n_outer, *refs), out_shape=(...]
    unnamed x12 -> x6, local copies, waits for them, and re-layouts: 6.48 us -> 3.04 us
where the time goes in v2:
time: 135 us; the launch traced here: 133 us
  Pallas kernels  126 us (93%)
  local copies, waits for them, and re-layouts  3.64 us (3%)
  between operations  1.95 us (1%)
    pallas_call x1, Pallas kernels, shards(): pl.pallas_call(lambda *refs: kernel(n_inner, n_outer, *refs), out_shape=(...  126 us
    unnamed x6, local copies, waits for them, and re-layouts  3.04 us

profile of v2, /device:TPU:1, one launch (start us, length us, event | category | flops | bytes accessed | tf_op | source)
XLA Modules:
  0.0 132.7 jit_solution(7755468164807215991)
XLA Ops:
  1.9 0.0 copy-start.1
  1.9 0.6 pad_maximum_fusion.refs_0_
  2.6 0.0 copy-done.1
  2.6 0.6 broadcast_in_dim.2.refs_5_
  3.2 126.5 %shard_map.86 = (f32[256,768]{1,0:T(8,128)}, f32[256,768]{1,0:T(8,128)}) custom-call(f32[2]{0:T(128)} %pad_maximum_fusion.refs_0_, bf16[256,1152]{1,0:T(8,128)(2,1)} %refs_1_.1, bf16[256,768]{1,0:T(8,128)(2,1)} %refs_2_.1, bf16[256,1152]{1,0:T(8,128)(2,1)} %refs_3_.1, bf16[256,768]{1,0:T(8,128)(2,1)} %refs_4_.1, s32[8,256]{1,0:T(8,128)} %broadcast_in_dim.2.refs_5_), custom_call_target="tpu_custom_call" | custom-call | flops 2264924160 | bytes 7077888 | tf_op jit(solution)/shard_map/pallas_call | solution.py:222
  129.7 0.0 copy-start
  129.7 2.1 %copy.13 = f32[256,768]{1,0:T(8,128)} copy(f32[256,768]{1,0:T(8,128)} %get-tuple-element.4) | data formatting | bytes 1572864
  131.8 0.0 copy-done
  131.8 0.9 copy.14
Async XLA Ops:
  1.9 0.7 copy-start.1
  129.7 2.1 %copy-start = (f32[256,768]{1,0:T(8,128)S(1)}, f32[256,768]{1,0:T(8,128)}, u32[]{:S(2)}) copy-start(f32[256,768]{1,0:T(8,128)} %get-tuple-element.5) | copy-start | bytes 2359300

commit v3 on v2

--- a/solution.py
+++ b/solution.py
@@ -20,6 +20,7 @@
     c = lax.rem(o, 2)
     at = lambda d: lax.rem(i + d + n_inner, n_inner)
     up, down = lax.rem(o + 1, n_outer), lax.rem(o + n_outer - 1, n_outer)
+    z = lax.rem(i, 6)
     rows = tm.shape[1]
 
     def copy(src, dst, ss, rs, dev):
@@ -44,6 +45,9 @@
     def text_next(k, dev):
         return text(k, k + 1, k, dev)
 
+    def text_over(d):
+        return text(0, d, 4, (at(d), o))
+
     def text_last(k, dev):
         return text(k, 4, 3, dev)
 
@@ -77,7 +81,12 @@
     @pl.when(c == 0)
     def _():
         signal((at(-3), down))
-        pl.semaphore_wait(barrier, 2)
+
+        @pl.when(z == 0)
+        def _():
+            signal((at(-3), o))
+
+        pl.semaphore_wait(barrier, 2 + z // 3 - z // 4)
 
     @pl.when(c == 1)
     def _():
@@ -106,24 +115,33 @@
 
     def step(s, carry):
         u = lax.rem(s // 2, 2)
-        a, b = c * u, s - 2 * c * u
+        a, b = c * u, s - c * u * (2 * s - 3)
+        label = s - c * u * (2 * s - 5)
 
         @pl.when((c == 0) & (s > 0) & (s < 3))
         def _():
             for w, cp in zip(text_next(s - 1, (i, o)), text_next(s, (at(1), o))):
                 w.wait_recv()
+
+                @pl.when((z <= 4) | (s == 1))
+                def _():
+                    cp.start()
+
+        @pl.when((c == 0) & (s == 3))
+        def _():
+            for w, cp in zip(text_next(2, (i, o)), text_last(3, (i, up))):
+                w.wait_recv()
                 cp.start()
 
-        @pl.when((c == 0) & (s == 3))
-        def _():
-            for w, cp in zip(text_next(2, (i, o)), text_last(3, (i, up))):
-                w.wait_recv()
+        @pl.when((c == 1) & (s == 1))
+        def _():
+            for w in text_next(0, (i, o)):
+                w.wait_recv()
+
+        @pl.when((c == 0) & (s == 3) & (z == 3))
+        def _():
+            for cp in text_over(3):
                 cp.start()
-
-        @pl.when((c == 1) & (s == 1))
-        def _():
-            for w in text_next(0, (i, o)):
-                w.wait_recv()
 
         if LATE == 1:
             @pl.when((c == 1) & (s == 1))
@@ -151,7 +169,7 @@
             il[a], tl[b], dims, preferred_element_type=jnp.float32) + offset
         r = lax.broadcasted_iota(jnp.int32, (rows, rows), 0)
         q = lax.broadcasted_iota(jnp.int32, (rows, rows), 1)
-        hit = (r == q) & (lk[a, 0:1, :] == s)
+        hit = (r == q) & (lk[a, 0:1, :] == label)
         target = 0.5 * (jnp.where(hit, 1.0, 0.0) + prob)
         g = (jax.nn.sigmoid(student) - target).astype(jnp.bfloat16)
         acc_img[a] += jnp.dot(g, tl[b], preferred_element_type=jnp.float32)
@@ -170,9 +188,12 @@
         def _():
             send_grad(3, 4, (i, up), acc_txt[3] + received(3))
 
+        @pl.when((c == 1) & (s == 2))
+        def _():
+            send_grad(1, 1, (at(-1), o), acc_txt[1])
+
         @pl.when((c == 1) & (s == 3))
         def _():
-            send_grad(1, 1, (at(-1), o), acc_txt[1])
             send_grad(4, 0, (at(2), o), acc_img[1])
             send_grad(0, 4, (at(3), up), acc_txt[0] + received(1))
 
@@ -200,7 +221,16 @@
 
     @pl.when(c == 0)
     def _():
-        sent(text_next(1, (i, o)) + text_next(2, (i, o)))
+        sent(text_next(1, (i, o)))
+
+        @pl.when(z <= 4)
+        def _():
+            sent(text_next(2, (i, o)))
+
+        @pl.when(z == 3)
+        def _():
+            sent(text_over(2))
+
         sent(grad(2, 4, (i, o)) + grad(3, 4, (i, o)))
 
     @pl.when(c == 1)
@@ -231,7 +261,7 @@
                 pltpu.VMEM((2, rows, ds), f32), pltpu.VMEM((5, rows, ds), f32),
                 pltpu.VMEM((5, rows, ds), WIRE), pltpu.VMEM((5, rows, ds), WIRE),
                 pltpu.VMEM((5, 8, 128), f32), pltpu.VMEM((5, 8, 128), f32),
-                dma((5,)), dma((4, PIECES)), dma((4, PIECES)), dma((5, PIECES)), dma((5, PIECES)),
+                dma((5,)), dma((5, PIECES)), dma((5, PIECES)), dma((5, PIECES)), dma((5, PIECES)),
                 dma((3,)), dma((3,)), dma((5,)), dma((5,)), dma((5,)), dma((5,)),
             ],
             compiler_params=pltpu.CompilerParams(

time: 135 us -> 134 us (level)
  no operation moved by 1% of the time
where the time goes in v3:
time: 134 us; the launch traced here: 133 us
  Pallas kernels  127 us (95%)
  local copies, waits for them, and re-layouts  3.64 us (3%)
  between operations  1.95 us (1%)
    pallas_call x1, Pallas kernels, shards(): pl.pallas_call(lambda *refs: kernel(n_inner, n_outer, *refs), out_shape=(...  127 us
    unnamed x6, local copies, waits for them, and re-layouts  3.04 us

profile of v3, /device:TPU:1, one launch (start us, length us, event | category | flops | bytes accessed | tf_op | source)
XLA Modules:
  0.0 132.8 jit_solution(3912589842105559000)
XLA Ops:
  1.9 0.0 copy-start.1
  1.9 0.6 pad_maximum_fusion.refs_0_
  2.6 0.0 copy-done.1
  2.6 0.6 broadcast_in_dim.2.refs_5_
  3.2 126.6 %shard_map.86 = (f32[256,768]{1,0:T(8,128)}, f32[256,768]{1,0:T(8,128)}) custom-call(f32[2]{0:T(128)} %pad_maximum_fusion.refs_0_, bf16[256,1152]{1,0:T(8,128)(2,1)} %refs_1_.1, bf16[256,768]{1,0:T(8,128)(2,1)} %refs_2_.1, bf16[256,1152]{1,0:T(8,128)(2,1)} %refs_3_.1, bf16[256,768]{1,0:T(8,128)(2,1)} %refs_4_.1, s32[8,256]{1,0:T(8,128)} %broadcast_in_dim.2.refs_5_), custom_call_target="tpu_custom_call" | custom-call | flops 2264924160 | bytes 7077888 | tf_op jit(solution)/shard_map/pallas_call | solution.py:252
  129.8 0.0 copy-start
  129.8 2.1 %copy.13 = f32[256,768]{1,0:T(8,128)} copy(f32[256,768]{1,0:T(8,128)} %get-tuple-element.4) | data formatting | bytes 1572864
  131.9 0.0 copy-done
  131.9 0.9 copy.14
Async XLA Ops:
  1.9 0.7 copy-start.1
  129.8 2.1 %copy-start = (f32[256,768]{1,0:T(8,128)S(1)}, f32[256,768]{1,0:T(8,128)}, u32[]{:S(2)}) copy-start(f32[256,768]{1,0:T(8,128)} %get-tuple-element.5) | copy-start | bytes 2359300

commit v4 on v3

--- a/solution.py
+++ b/solution.py
@@ -39,8 +39,8 @@
     ]
     def text(k, to, sem, dev):
         n = rows // PIECES
-        return [copy(buf.at[k, pl.ds(q * n, n)], buf.at[to, pl.ds(q * n, n)], ss.at[sem, q], rs.at[to, q], dev)
-                for buf, ss, rs in ((tm, tm_s, tm_r), (tl, tl_s, tl_r)) for q in range(PIECES)]
+        return [copy((own if isinstance(k, int) and k == 0 else buf.at[k]).at[pl.ds(q * n, n)], buf.at[to, pl.ds(q * n, n)], ss.at[sem, q], rs.at[to, q], dev)
+                for buf, own, ss, rs in ((tm, mt, tm_s, tm_r), (tl, lt, tl_s, tl_r)) for q in range(PIECES)]
 
     def text_next(k, dev):
         return text(k, k + 1, k, dev)
@@ -53,9 +53,9 @@
 
     def image_back():
         dev = (at(-2), o)
-        return (copy(im.at[0], im.at[1], i_s.at[0], i_r.at[0], dev),
-                copy(il.at[0], il.at[1], i_s.at[1], i_r.at[1], dev),
-                copy(lk.at[0], lk.at[1], i_s.at[2], i_r.at[2], dev))
+        return (copy(mi, im.at[1], i_s.at[0], i_r.at[0], dev),
+                copy(li, il.at[1], i_s.at[1], i_r.at[1], dev),
+                copy(look, lk.at[1], i_s.at[2], i_r.at[2], dev))
 
     def grad(k, slot, dev):
         return (copy(msend.at[k], mrecv.at[slot], m_s.at[k], m_r.at[slot], dev),
@@ -96,8 +96,6 @@
         signal((i, down))
         pl.semaphore_wait(barrier, 5)
 
-    for cp in local:
-        cp.wait()
     for cp in text_next(0, (at(1), o)):
         cp.start()
 
@@ -112,6 +110,8 @@
     acc_img[...] = jnp.zeros_like(acc_img)
     acc_txt[...] = jnp.zeros_like(acc_txt)
     sharp, offset = scalars[0], scalars[1]
+    for cp in local:
+        cp.wait()
 
     def step(s, carry):
         u = lax.rem(s // 2, 2)

time: 134 us -> 134 us (level)
  no operation moved by 1% of the time
where the time goes in v4:
time: 134 us; the launch traced here: 133 us
  Pallas kernels  127 us (95%)
  local copies, waits for them, and re-layouts  3.64 us (3%)
  between operations  1.95 us (1%)
    pallas_call x1, Pallas kernels, shards(): pl.pallas_call(lambda *refs: kernel(n_inner, n_outer, *refs), out_shape=(...  127 us
    unnamed x6, local copies, waits for them, and re-layouts  3.04 us

profile of v4, /device:TPU:1, one launch (start us, length us, event | category | flops | bytes accessed | tf_op | source)
XLA Modules:
  0.0 133.0 jit_solution(12448030610659174495)
XLA Ops:
  1.9 0.0 copy-start.1
  1.9 0.6 pad_maximum_fusion.refs_0_
  2.6 0.0 copy-done.1
  2.6 0.6 broadcast_in_dim.2.refs_5_
  3.2 126.8 %shard_map.86 = (f32[256,768]{1,0:T(8,128)}, f32[256,768]{1,0:T(8,128)}) custom-call(f32[2]{0:T(128)} %pad_maximum_fusion.refs_0_, bf16[256,1152]{1,0:T(8,128)(2,1)} %refs_1_.1, bf16[256,768]{1,0:T(8,128)(2,1)} %refs_2_.1, bf16[256,1152]{1,0:T(8,128)(2,1)} %refs_3_.1, bf16[256,768]{1,0:T(8,128)(2,1)} %refs_4_.1, s32[8,256]{1,0:T(8,128)} %broadcast_in_dim.2.refs_5_), custom_call_target="tpu_custom_call" | custom-call | flops 2264924160 | bytes 7077888 | tf_op jit(solution)/shard_map/pallas_call | solution.py:252
  130.0 0.0 copy-start
  130.0 2.1 %copy.13 = f32[256,768]{1,0:T(8,128)} copy(f32[256,768]{1,0:T(8,128)} %get-tuple-element.4) | data formatting | bytes 1572864
  132.1 0.0 copy-done
  132.1 0.9 copy.14
Async XLA Ops:
  1.9 0.7 copy-start.1
  130.0 2.1 %copy-start = (f32[256,768]{1,0:T(8,128)S(1)}, f32[256,768]{1,0:T(8,128)}, u32[]{:S(2)}) copy-start(f32[256,768]{1,0:T(8,128)} %get-tuple-element.5) | copy-start | bytes 2359300
